TPU v7x, 32 devices: a whole 2x2x4 slice. The times are simulated.
32 devices in a mesh: groups: 2 (over y), seq: 4 (over z), req: 2 (over x), head: 2 (over core).
Axes of the slice: x: 2, y: 2, z: 4, core: 2. Of those that a mesh axis runs over, the one named last changes fastest.
Arguments:
- cache: bfloat16 [8, 6144, 576], P(('groups', 'req'), 'seq'), parts along dimension 0, may hold values from -4 to 4
- index_key: bfloat16 [8, 6144, 128], P(('groups', 'req'), 'seq'), parts along dimension 0, may hold values from -4 to 4
- index_scale: float32 [8, 6144], P(('groups', 'req'), 'seq'), parts along dimension 0, may hold values from 1.5 to 12
- lengths: int32 [8], P(('groups', 'req')), parts along dimension 0, may hold values from 4608 to 6143, as said below
- owners: int32 [8], P(('groups', 'req')), parts along dimension 0, may hold values from 0 to 3, as said below
- selected: int32 [2, 8, 2048], P(None, ('groups', 'req')), parts along dimension 1, may hold values from 0 to 6143, as said below
- query: bfloat16 [2, 16, 128, 576], P(None, ('groups', 'seq', 'req'), 'head'), parts along dimension 1, may hold values from -41 to 41
- index_query: bfloat16 [2, 16, 64, 128], P(None, ('groups', 'seq', 'req')), parts along dimension 1, may hold values from -0.5 to 0.5
- index_weight: bfloat16 [2, 16, 64], P(None, ('groups', 'seq', 'req')), parts along dimension 1, may hold values from -0.75 to 0.75
Outputs:
- index_scores: float32 [2, 8, 6144], P(None, ('groups', 'req'), 'seq'), parts along dimension 1
- threshold: float32 [2, 8], P(None, ('groups', 'req')), parts along dimension 1
- attended: bfloat16 [2, 16, 128, 512], P(None, ('groups', 'seq', 'req'), 'head'), parts along dimension 1
There are 2 independent parts, one for each index of `groups`. A program takes and returns all parts, laid end to end along the dimension named above; each array names one. Nothing has to cross between parts.
Inputs may be any that keep to these rules, and one draw needn't show every extreme that they name: `lengths`: some request of each group has length 6143. The 2 requests i * 2 to (i + 1) * 2 - 1 have distinct owners. selected[t, r] holds 2048 distinct positions below lengths[r] + t; at most 768 of them lie in one block of positions k * 1536 to (k + 1) * 1536 - 1, and in every list some block holds exactly 768.
All inputs are finite; a program needn't handle non-finite values.
Results may differ from a plain program's by a relative error of at most 0.007.
Values may be sent and summed in bfloat16 or wider, within the bound.
A program may use at most 64 MiB of HBM per device.

v0:
```python
import jax
import jax.numpy as jnp
from jax import lax
from jax.sharding import PartitionSpec as P

ROPE = 64


score_scale = 192.0 ** (-0.5)
masked_value = -1e30


def combined_all(x, axis, join):
    gathered = lax.all_gather(x.astype(jnp.bfloat16), axis)

    def take(source):
        return lax.dynamic_index_in_dim(gathered, source, 0, False).astype(x.dtype)

    return lax.fori_loop(
        1, lax.axis_size(axis), lambda source, state: join(state, take(source)), take(0)
    )


def top_values(earlier, later):
    keep_count = earlier.shape[-1]
    return lax.top_k(jnp.concatenate([earlier, later], axis=-1), keep_count)[0]


def shards(
    cache, index_key, index_scale, lengths, owners, selected, query, index_query, index_weight
):
    seq_count = lax.axis_size("seq")
    seq_rank = lax.axis_index("seq")
    local_requests = cache.shape[0]
    shard_rows = cache.shape[1]
    row_width = cache.shape[2]
    step_count = selected.shape[0]
    select_count = selected.shape[2]
    latent_width = row_width - ROPE
    capacity = shard_rows // 2
    step_ids = jnp.arange(step_count, dtype=jnp.int32)
    seq_ids = jnp.arange(seq_count, dtype=jnp.int32)
    request_ids = jnp.arange(local_requests, dtype=jnp.int32)
    owner_table = owners[:, None] == seq_ids[None, :]
    picker = owner_table.astype(jnp.bfloat16)
    dest_request = jnp.sum(owner_table.astype(jnp.int32) * request_ids[:, None], axis=0)
    owned_here = owners == seq_rank
    holds_request = jnp.any(owned_here)
    heads_query, heads_weight = (
        lax.all_gather(index_query, "seq", axis=1, tiled=True),
        lax.all_gather(index_weight, "seq", axis=1, tiled=True),
    )
    owner_query = jnp.einsum(
        "jo,tohd->tjhd", picker, heads_query, preferred_element_type=jnp.float32
    ).astype(jnp.bfloat16)
    owner_weight = jnp.einsum(
        "jo,toh->tjh", picker, heads_weight, preferred_element_type=jnp.float32
    )
    raw_dots = jnp.einsum(
        "tjhd,jpd->tjhp", owner_query, index_key, preferred_element_type=jnp.float32
    )
    scores = jnp.sum(jax.nn.relu(raw_dots) * owner_weight[..., None], axis=2) * index_scale[None]
    positions = seq_rank * shard_rows + jnp.arange(shard_rows, dtype=jnp.int32)
    in_length = positions[None, None, :] < lengths[None, :, None] + step_ids[:, None, None]
    index_scores = jnp.where(in_length, scores, 0.0)
    candidates = jnp.where(in_length, scores, masked_value)
    candidates = jnp.pad(
        candidates, ((0, 0), (0, 0), (0, select_count - shard_rows)), constant_values=masked_value
    )
    ranked = combined_all(candidates, "seq", top_values)
    threshold = ranked[..., select_count - 1]
    owning = selected // shard_rows == seq_rank
    placing = jnp.cumsum(owning.astype(jnp.int32), axis=2) - 1
    counts = jnp.sum(owning.astype(jnp.int32), axis=2)
    target = jnp.where(owning, placing, capacity)
    local_position = selected - seq_rank * shard_rows
    step_grid = jnp.broadcast_to(step_ids[:, None, None], selected.shape)
    request_grid = jnp.broadcast_to(request_ids[None, :, None], selected.shape)
    slot_position = jnp.zeros((step_count, local_requests, capacity + 1), jnp.int32)
    slot_position = slot_position.at[step_grid, request_grid, target].set(local_position)[
        :, :, :capacity
    ]
    flat_cache = cache.reshape(local_requests * shard_rows, row_width)
    slot_ids = jnp.arange(capacity, dtype=jnp.int32)
    all_queries = lax.all_gather(query, "seq", axis=1, tiled=True)
    request_query = jnp.einsum(
        "jo,tohd->tjhd", picker, all_queries, preferred_element_type=jnp.float32
    ).astype(jnp.bfloat16)
    local_rows = jnp.take(
        flat_cache, request_ids[None, :, None] * shard_rows + slot_position, axis=0
    )
    usable = (slot_ids[None, None, :] < counts[:, :, None])[:, :, None, :]
    logits = (
        jnp.einsum("tjhd,tjcd->tjhc", request_query, local_rows, preferred_element_type=jnp.float32)
        * score_scale
    )
    logits = jnp.where(usable, logits, masked_value)
    row_peak = jnp.max(logits, axis=3)
    weights = jnp.where(usable, jnp.exp(logits - row_peak[..., None]), 0.0)
    row_total = jnp.sum(weights, axis=3)
    mixture = jnp.einsum(
        "tjhc,tjcd->tjhd",
        weights.astype(jnp.bfloat16),
        local_rows,
        preferred_element_type=jnp.float32,
    )[..., :latent_width]
    outbound = (
        jnp.take(mixture, dest_request, axis=1),
        jnp.take(row_peak, dest_request, axis=1),
        jnp.take(row_total, dest_request, axis=1),
    )
    got_mixture, got_peak, got_total = (
        lax.all_to_all(outbound[0], "seq", split_axis=1, concat_axis=1, tiled=True),
        lax.all_to_all(outbound[1], "seq", split_axis=1, concat_axis=1, tiled=True),
        lax.all_to_all(outbound[2], "seq", split_axis=1, concat_axis=1, tiled=True),
    )
    highest = jnp.max(got_peak, axis=1, keepdims=True)
    rescale = jnp.exp(got_peak - highest)
    merged = jnp.sum(got_mixture * rescale[..., None], axis=1)
    result = merged / jnp.sum(got_total * rescale, axis=1)[..., None]
    attended = jnp.where(holds_request, result, 0.0).astype(jnp.bfloat16)[:, None]
    return (index_scores, threshold, attended)


def solution(mesh):
    placed = (
        P(("groups", "req"), "seq", None),
        P(("groups", "req"), "seq", None),
        P(("groups", "req"), "seq"),
        P(("groups", "req")),
        P(("groups", "req")),
        P(None, ("groups", "req"), None),
        P(None, ("groups", "seq", "req"), "head", None),
        P(None, ("groups", "seq", "req"), None, None),
        P(None, ("groups", "seq", "req"), None),
    )
    return jax.shard_map(
        shards,
        mesh=mesh,
        in_specs=placed,
        out_specs=(
            P(None, ("groups", "req"), "seq"),
            P(None, ("groups", "req")),
            P(None, ("groups", "seq", "req"), "head", None),
        ),
        check_vma=False,
    )
```

profile of v0, /device:TPU:0, one launch (start us, length us, event | category | flops | bytes accessed | tf_op | source)
XLA Modules:
  0.0 209.8 jit_solution(12546323164927925906)
XLA Ops:
  0.6 0.0 copy-start
  0.7 0.8 select_reduce_fusion
  1.5 1.0 convert_reduce_fusion
  2.5 1.2 reduce-window.6
  3.7 0.2 slice_reduce_fusion
  3.9 0.4 reduce-window.9
  4.3 0.1 add_add_fusion
  4.5 0.8 multiply_reduce_fusion.1
  5.3 0.8 and_reduce_fusion
  6.2 30.5 %scatter_custom_fusion = s32[3076]{0:T(1024)S(1)} fusion(s32[8192]{0:T(1024)S(1)} %bitcast.77, s32[8192]{0:T(1024)S(1)} %bitcast.78, s32[]{:T(128)} %constant.120.clone.1), kind=kCustom, calls=%fused_computation.56 | custom fusion | bytes 12308
  36.6 0.1 reshape.114
  36.7 0.1 compare_and_fusion
  36.9 5.9 %copy.42 = bf16[2,1536,576]{2,1,0:T(8,128)(2,1)} copy(bf16[2,1536,576]{1,2,0:T(8,128)(2,1)} %param.13) | data formatting | bytes 7077888 | tf_op args[0]
  42.8 16.4 %gather_fusion = bf16[3072,576]{1,0:T(8,128)(2,1)} fusion(bf16[3072,576]{1,0:T(8,128)(2,1)} %bitcast.72, s32[3072]{0:T(1024)S(1)} %broadcast_clamp_fusion), kind=kCustom, calls=%fused_computation.2 | custom fusion | bytes 7090176 | tf_op jit(solution)/shard_map/jit(_take)/gather | solution.py:89
  59.2 6.2 %copy.43 = bf16[2,2,768,576]{2,3,1,0:T(8,128)(2,1)} copy(bf16[2,2,768,576]{3,2,1,0:T(8,128)(2,1)} %bitcast.73) | data formatting | bytes 7077888 | tf_op jit(solution)/shard_map/jit(_take)/gather | solution.py:89
  65.4 0.1 iota_compare_fusion
  65.5 0.0 copy-done.2
  65.5 19.6 %all_gather.19 = bf16[2,4,64,576]{3,2,0,1:T(8,128)(2,1)S(1)} all-gather(bf16[2,1,64,576]{3,2,0,1:T(8,128)(2,1)S(1)} %bitcast.75), channel_id=1, replica_groups=mesh['groups'=2,'seq'=4,'req'=2,'head'=2] {'seq'}, dimensions={1}, use_global_device_ids=true | all-gather | bytes 737280 | tf_op jit(solution)/shard_map/all_gather | solution.py:85
  85.1 0.0 copy-done.7
  85.1 0.6 fusion.6
  85.7 2.3 %broadcast_select_fusion = bf16[2,2,768,576]{2,3,1,0:T(8,128)(2,1)S(1)} fusion(bf16[2,2,768,576]{2,3,1,0:T(8,128)(2,1)} %copy.43, pred[2,2,768]{2,1,0:T(4,128)(4,1)S(1)} %get-tuple-element.111), kind=kLoop, calls=%fused_computation.7 | loop fusion | flops 1769472 | bytes 7080960 | tf_op jit(solution)/shard_map/jit(_take)/select_n | solution.py:89
  88.1 0.0 copy-start.1
  88.1 1.7 copy-done.1
  89.8 0.9 fusion.36
  90.7 0.0 copy-start.5
  90.7 0.0 copy-start.6
  90.7 0.3 fusion.10
  91.0 0.0 copy-start.4
  91.1 0.6 gather_fusion.3
  91.6 0.6 gather_fusion.2
  92.2 0.1 select_bitcast_fusion.3
  92.3 0.7 reshape.174
  93.0 3.9 %all-to-all-start.1 = ((f32[4,1,128]{2,1,0:T(1,128)}), f32[4,1,128]{2,1,0:T(1,128)S(1)}, u32[]{:S(2)}, u32[]{:S(2)}) async-start(f32[4,1,128]{2,1,0:T(1,128)} %reshape.174), calls=%async_computation.1 | async-start | bytes 4096 | tf_op jit(solution)/shard_map/all_to_all | solution.py:114
  96.9 3.0 %fusion = f32[2,2,64,512]{3,2,1,0:T(8,128)S(1)} fusion(bf16[2,2,768,576]{2,3,1,0:T(8,128)(2,1)} %copy-done.1, f32[2,2,64,768]{3,2,1,0:T(8,128)S(1)} %get-tuple-element.119, f32[2,2,64]{2,1,0:T(2,128)S(1)} %get-tuple-element.118, pred[2,2,768]{2,1,0:T(4,128)(4,1)S(1)} %iota_compare_fusion), kind=kOutput, calls=%fused_computation.8 | convolution fusion | flops 201916416 | bytes 4460544 | tf_op jit(solution)/shard_map/tjhc,tjcd->tjhd/dot_general | solution.py:101
  99.9 13.9 %all_gather.15 = bf16[2,4,64,128]{3,2,0,1:T(8,128)(2,1)S(1)} all-gather(bf16[2,1,64,128]{3,2,0,1:T(8,128)(2,1)S(1)} %bitcast.76), channel_id=1, replica_groups=mesh['groups'=2,'seq'=4,'req'=2,'head'=2] {'seq'}, dimensions={1}, use_global_device_ids=true | all-gather | bytes 163840 | tf_op jit(solution)/shard_map/all_gather | solution.py:50
  113.8 0.3 fusion.7
  114.1 10.8 %all_gather.16 = bf16[2,4,64]{2,0,1:T(2,128)(2,1)S(1)} all-gather(bf16[2,1,64]{2,0,1:T(2,128)(2,1)S(1)} %copy-done.5), channel_id=1, replica_groups=mesh['groups'=2,'seq'=4,'req'=2,'head'=2] {'seq'}, dimensions={1}, use_global_device_ids=true | all-gather | bytes 1280 | tf_op jit(solution)/shard_map/all_gather | solution.py:51
  124.9 0.2 convolution_bitcast_fusion
  125.1 0.1 iota_add_fusion.1
  125.2 0.4 fusion.4
  125.6 0.1 fusion.23
  125.7 13.1 %all-gather = bf16[8,2,2048]{2,1,0:T(2,128)(2,1)S(1)} all-gather(bf16[2,2,2048]{2,1,0:T(2,128)(2,1)S(1)} %pad.5.clone), channel_id=2, replica_groups=mesh['groups'=2,'seq'=4,'req'=2,'head'=2] {'seq'}, dimensions={0}, use_global_device_ids=true | all-gather | bytes 81920 | tf_op jit(solution)/shard_map/all_gather | solution.py:14
  138.8 0.6 gather_fusion.1
  139.5 1.2 select_bitcast_fusion
  140.7 0.7 reshape.176
  141.3 0.0 all-to-all-done.1
  141.3 3.2 %all-to-all-start.2 = ((f32[4,1,128]{2,1,0:T(1,128)}), f32[4,1,128]{2,1,0:T(1,128)S(1)}, u32[]{:S(2)}, u32[]{:S(2)}) async-start(f32[4,1,128]{2,1,0:T(1,128)} %reshape.176), calls=%async_computation.2 | async-start | bytes 4096 | tf_op jit(solution)/shard_map/all_to_all | solution.py:115
  144.6 0.7 compare_reduce_fusion
  145.3 0.6 copy.47
  145.9 4.2 %all-to-all-done.2 = f32[4,1,128]{2,1,0:T(1,128)S(1)} async-done(((f32[4,1,128]{2,1,0:T(1,128)}), f32[4,1,128]{2,1,0:T(1,128)S(1)}, u32[]{:S(2)}, u32[]{:S(2)}) %all-to-all-start.2) | async-done | bytes 2080 | tf_op jit(solution)/shard_map/all_to_all | solution.py:115
  150.1 5.6 %all-to-all-start = ((f32[2,4,64,512]{3,2,0,1:T(8,128)}), f32[2,4,64,512]{3,2,0,1:T(8,128)S(1)}, u32[]{:S(2)}, u32[]{:S(2)}) async-start(f32[2,4,64,512]{3,2,0,1:T(8,128)} %select_bitcast_fusion), calls=%async_computation | async-start | bytes 2097152 | tf_op jit(solution)/shard_map/all_to_all | solution.py:113
  155.7 49.8 %while.15 = (s32[]{:T(128)}, f32[2,2,2048]{2,1,0:T(2,128)S(1)}, bf16[4,2,2,2048]{3,2,1,0:T(2,128)(2,1)S(1)}, s32[]{:T(128)}, s32[]{:T(128)}, /*index=5*/s32[]{:T(128)}) while((s32[]{:T(128)}, f32[2,2,2048]{2,1,0:T(2,128)S(1)}, bf16[4,2,2,2048]{3,2,1,0:T(2,128)(2,1)S(1)}, s32[]{:T(128)}, s32[]{:T(128)}, /*index=5*/s32[]{:T(128)}) %tuple.53), condition=%wide.region_3.4_spmd, body=%wide.region_1.3_spmd.sunk | while | flops 253957 | bytes 573555 | solution.py:19
  155.8 16.5 %top_k.11 = (f32[2,2,4096]{2,1,0:T(2,128)S(1)}, s32[2,2,4096]{2,1,0:T(2,128)}) sort(f32[2,2,4096]{2,1,0:T(2,128)S(1)} %pad_maximum_fusion.2, s32[2,2,4096]{2,1,0:T(2,128)S(1)} %iota.45), dimensions={2}, to_apply=%region_2.2 | sort | flops 229376 | bytes 262144 | tf_op jit(solution)/shard_map/while/body/eval_jaxpr/top_k | solution.py:26
  172.4 16.5 %top_k.11 = (f32[2,2,4096]{2,1,0:T(2,128)S(1)}, s32[2,2,4096]{2,1,0:T(2,128)}) sort(f32[2,2,4096]{2,1,0:T(2,128)S(1)} %pad_maximum_fusion.2, s32[2,2,4096]{2,1,0:T(2,128)S(1)} %iota.45), dimensions={2}, to_apply=%region_2.2 | sort | flops 229376 | bytes 262144 | tf_op jit(solution)/shard_map/while/body/eval_jaxpr/top_k | solution.py:26
  188.9 16.5 %top_k.11 = (f32[2,2,4096]{2,1,0:T(2,128)S(1)}, s32[2,2,4096]{2,1,0:T(2,128)}) sort(f32[2,2,4096]{2,1,0:T(2,128)S(1)} %pad_maximum_fusion.2, s32[2,2,4096]{2,1,0:T(2,128)S(1)} %iota.45), dimensions={2}, to_apply=%region_2.2 | sort | flops 229376 | bytes 262144 | tf_op jit(solution)/shard_map/while/body/eval_jaxpr/top_k | solution.py:26
  205.4 0.7 slice_reduce_fusion.1
  206.2 0.5 broadcast.224
  206.7 0.7 reduce.8
  207.3 0.1 reshape.175
  207.4 0.7 reduce.9
  208.1 0.1 reshape.177
  208.2 0.0 all-to-all-done
  208.2 0.1 multiply_reduce_fusion
  208.4 1.4 fusion.18
  (46 shorter events, 0.5 us)
Async XLA Ops:
  0.6 124.5 %copy-start = (bf16[2,1536,128]{2,1,0:T(8,128)(2,1)S(1)}, bf16[2,1536,128]{2,1,0:T(8,128)(2,1)}, u32[]{:S(2)}) copy-start(bf16[2,1536,128]{2,1,0:T(8,128)(2,1)} %param.14) | copy-start | bytes 2359300
  59.2 6.3 %copy-start.2 = (bf16[2,1,64,576]{3,2,1,0:T(8,128)(2,1)S(1)}, bf16[2,1,64,576]{3,2,1,0:T(8,128)(2,1)}, u32[]{:S(2)}) copy-start(bf16[2,1,64,576]{3,2,1,0:T(8,128)(2,1)} %param.19) | copy-start | bytes 442372
  59.2 25.9 %copy-start.7 = (s32[2]{0:T(128)S(1)}, s32[2]{0:T(128)}, u32[]{:S(2)}) copy-start(s32[2]{0:T(128)} %param.17) | copy-start | bytes 28
  88.1 1.8 copy-start.1
  90.7 9.2 %copy-start.3 = (bf16[2,1,64,128]{3,2,1,0:T(8,128)(2,1)S(1)}, bf16[2,1,64,128]{3,2,1,0:T(8,128)(2,1)}, u32[]{:S(2)}) copy-start(bf16[2,1,64,128]{3,2,1,0:T(8,128)(2,1)} %param.20) | copy-start | bytes 98308
  90.7 23.4 %copy-start.5 = (bf16[2,1,64]{2,0,1:T(2,128)(2,1)S(1)}, bf16[2,1,64]{2,0,1:T(2,128)(2,1)}, u32[]{:S(2)}) copy-start(bf16[2,1,64]{2,0,1:T(2,128)(2,1)} %param.21) | copy-start | bytes 772
  90.7 34.4 %copy-start.6 = (s32[2]{0:T(128)S(1)}, s32[2]{0:T(128)}, u32[]{:S(2)}) copy-start(s32[2]{0:T(128)} %param.16) | copy-start | bytes 28
  91.0 34.5 %copy-start.4 = (f32[2,1536]{1,0:T(2,128)S(1)}, f32[2,1536]{1,0:T(2,128)}, u32[]{:S(2)}) copy-start(f32[2,1536]{1,0:T(2,128)} %param.15) | copy-start | bytes 36868
  93.0 48.4 %all-to-all-start.1 = ((f32[4,1,128]{2,1,0:T(1,128)}), f32[4,1,128]{2,1,0:T(1,128)S(1)}, u32[]{:S(2)}, u32[]{:S(2)}) async-start(f32[4,1,128]{2,1,0:T(1,128)} %reshape.174), calls=%async_computation.1 | async-start | bytes 4096 | tf_op jit(solution)/shard_map/all_to_all | solution.py:114
  141.3 8.7 %all-to-all-start.2 = ((f32[4,1,128]{2,1,0:T(1,128)}), f32[4,1,128]{2,1,0:T(1,128)S(1)}, u32[]{:S(2)}, u32[]{:S(2)}) async-start(f32[4,1,128]{2,1,0:T(1,128)} %reshape.176), calls=%async_computation.2 | async-start | bytes 4096 | tf_op jit(solution)/shard_map/all_to_all | solution.py:115
  150.1 58.1 %all-to-all-start = ((f32[2,4,64,512]{3,2,0,1:T(8,128)}), f32[2,4,64,512]{3,2,0,1:T(8,128)S(1)}, u32[]{:S(2)}, u32[]{:S(2)}) async-start(f32[2,4,64,512]{3,2,0,1:T(8,128)} %select_bitcast_fusion), calls=%async_computation | async-start | bytes 2097152 | tf_op jit(solution)/shard_map/all_to_all | solution.py:113
where the time goes:
time: 211 us; the launch traced here: 210 us
  local copies, waits for them, and re-layouts  66.4 us (31%)
  other arithmetic  62.7 us (30%)
  blocking collectives  57.5 us (27%)
  starting transfers between devices  12.7 us (6%)
  matrix products  5.34 us (3%)
  waiting for transfers between devices  4.18 us (2%)
    top_k x3, other arithmetic, top_values(): return lax.top_k(jnp.concatenate([earlier, later], axis=-1), keep_count)[0]  49.5 us
    unnamed x26, local copies, waits for them, and re-layouts  40.3 us
    gather x2, local copies, waits for them, and re-layouts, shards(): jnp.take(flat_cache, request_ids[None, :, None] * shard_rows + slot_posit...  22.6 us
    all_gather x1, blocking collectives, shards(): all_queries = lax.all_gather(query, 'seq', axis=1, tiled=True)  19.6 us
    all_gather x1, blocking collectives, shards(): lax.all_gather(index_query, 'seq', axis=1, tiled=True)  13.9 us
    all_gather x1, blocking collectives, combined_all(): gathered = lax.all_gather(x.astype(jnp.bfloat16), axis)  13.1 us
    all_gather x1, blocking collectives, shards(): lax.all_gather(index_weight, 'seq', axis=1, tiled=True)  10.8 us
    all_to_all x1, starting transfers between devices, shards(): lax.all_to_all(outbound[0], 'seq', split_axis=1, concat_axis=1, tiled=True)  5.61 us
  transfers between devices with their start and end apart: 3, of which 1 were waited for; matrix products, arithmetic and copies ran while one was open for 29% of the time, Pallas kernels for 0%

commit v1 on v0

v1 whole, which is shorter than its diff:
```python
import functools

import jax
import jax.numpy as jnp
from jax import lax
from jax.experimental import pallas as pl
from jax.experimental.pallas import tpu as pltpu
from jax.sharding import PartitionSpec as P

ROPE = 64
LANES = 128
PIVOTS = 7
ROUNDS = 11

score_scale = 192.0 ** (-0.5)
masked_value = -1e30
NT = (((1,), (1,)), ((), ()))
NN = (((1,), (0,)), ((), ()))


def dot(a, b, dims):
    return lax.dot_general(a, b, dims, preferred_element_type=jnp.float32)


def iota(shape, dim):
    return lax.broadcasted_iota(jnp.int32, shape, dim)


def to_column(row):
    n = row.shape[1]
    eye = iota((n, n), 0) == iota((n, n), 1)
    return jnp.sum(jnp.where(eye, row, 0.0), axis=1, keepdims=True)


def to_row(column):
    n = column.shape[0]
    eye = iota((n, n), 0) == iota((n, n), 1)
    return jnp.sum(jnp.where(eye, column, 0.0), axis=0, keepdims=True)


def kernel(
    n,
    lengths,
    owners,
    cache_hbm,
    key_hbm,
    scale_ref,
    selected_ref,
    query_ref,
    iq_ref,
    iw_ref,
    scores_out,
    threshold_out,
    attended_out,
    cache_v,
    key_v,
    iq_all,
    q_all,
    cand,
    bias,
    mix_out,
    stat_out,
    mix_in,
    stat_in,
    local_sem,
    iq_send,
    iq_recv,
    q_send,
    q_recv,
    c_send,
    c_recv,
    m_send,
    m_recv,
    s_send,
    s_recv,
):
    me = lax.axis_index("seq")
    steps, reqs, picks = selected_ref.shape
    rows = cache_v.shape[1]
    heads = query_ref.shape[2]
    latent = mix_in.shape[2]
    iheads = iq_ref.shape[2]
    crow = cand.shape[1]
    fold = crow // (steps * reqs)

    key_copy = pltpu.make_async_copy(key_hbm, key_v, local_sem.at[0])
    cache_copy = pltpu.make_async_copy(cache_hbm, cache_v, local_sem.at[1])
    key_copy.start()
    cache_copy.start()

    def peer(d):
        return lax.rem(me + d, n)

    def remote(src, dst, send, recv, d):
        return pltpu.make_async_remote_copy(
            src_ref=src,
            dst_ref=dst,
            send_sem=send.at[peer(d)],
            recv_sem=recv,
            device_id={"seq": peer(d)},
            device_id_type=pl.DeviceIdType.MESH,
        )

    barrier = pltpu.get_barrier_semaphore()
    for d in range(1, n):
        pl.semaphore_signal(
            barrier, inc=1, device_id={"seq": peer(d)}, device_id_type=pl.DeviceIdType.MESH
        )
    for t in range(steps):
        iq_all[me, t * iheads : (t + 1) * iheads, :] = iq_ref[t, 0]
    wide = jnp.concatenate([iw_ref[t] for t in range(steps)], axis=0).astype(jnp.float32)
    iq_all[me, steps * iheads :, :] = jnp.pad(
        wide, ((0, 16 - steps), (0, LANES - iheads))
    ).astype(jnp.bfloat16)
    q_all[me] = query_ref[:, 0]
    pl.semaphore_wait(barrier, n - 1)

    for d in range(1, n):
        remote(iq_all.at[me], iq_all.at[me], iq_send, iq_recv.at[me], d).start()
    for d in range(1, n):
        remote(q_all.at[me], q_all.at[me], q_send, q_recv.at[me], d).start()

    base = me * rows
    blocks = rows // LANES
    hi_rows = -(-blocks // 16) * 16
    for j in range(reqs):
        for t in range(steps):
            local = selected_ref[t, j : j + 1, :] - base
            hi = jnp.right_shift(local, 7)
            lo = jnp.bitwise_and(local, LANES - 1)
            hot_hi = jnp.where(iota((hi_rows, picks), 0) == hi, 1.0, 0.0).astype(jnp.bfloat16)
            hot_lo = jnp.where(iota((LANES, picks), 0) == lo, 1.0, 0.0).astype(jnp.bfloat16)
            hits = dot(hot_hi, hot_lo, NT)
            row = jnp.concatenate([hits[b : b + 1] for b in range(blocks)], axis=1)
            bias[j, t : t + 1, :] = jnp.where(row > 0.5, 0.0, masked_value)

    key_copy.wait()
    for d in range(1, n):
        remote(iq_all.at[peer(d)], iq_all.at[peer(d)], iq_send, iq_recv.at[peer(d)], d).wait_recv()
    position = base + iota((1, rows), 1)
    part = rows // fold
    for j in range(reqs):
        packed = iq_all[owners[j]]
        dots = jnp.maximum(dot(packed[: steps * iheads], key_v[j], NT), 0.0)
        scale = scale_ref[j : j + 1, :]
        for t in range(steps):
            w = packed[steps * iheads :].astype(jnp.float32)[t : t + 1, :iheads]
            total = jnp.sum(
                dots[t * iheads : (t + 1) * iheads] * to_column(w), axis=0, keepdims=True
            )
            total = total * scale
            inside = position < lengths[j] + t
            scores_out[t, j : j + 1, :] = jnp.where(inside, total, 0.0)
            candidates = jnp.where(inside, total, masked_value)
            for f in range(fold):
                at = f * steps * reqs + t * reqs + j
                cand[me, at : at + 1, :] = candidates[:, f * part : (f + 1) * part]
    for d in range(1, n):
        remote(cand.at[me], cand.at[me], c_send, c_recv.at[me], d).start()

    cache_copy.wait()

    def unit(s):
        j = jnp.int32(0)
        for r in range(reqs):
            j = j + jnp.where(owners[r] == s, r, 0)
        latents = cache_v[j]
        logits = dot(q_all[s].reshape(steps * heads, -1), latents, NT) * score_scale
        mask = bias[j]
        logits = jnp.concatenate(
            [logits[t * heads : (t + 1) * heads] + mask[t : t + 1] for t in range(steps)], axis=0
        )
        peak = jnp.max(logits, axis=1, keepdims=True)
        weights = jnp.exp(logits - peak)
        total = jnp.sum(weights, axis=1, keepdims=True)
        mixture = dot(weights.astype(jnp.bfloat16), latents[:, :latent], NN) / total
        stat = jnp.concatenate([to_row(peak), to_row(total)], axis=0)
        return mixture.astype(jnp.bfloat16), jnp.pad(stat, ((0, 6), (0, 0)))

    mix_in[me], stat_in[me] = unit(me)

    def send_unit(d, carry):
        s = peer(d)
        remote(q_all.at[s], q_all.at[s], q_send, q_recv.at[s], d).wait_recv()
        mix_out[s], stat_out[s] = unit(s)
        remote(mix_out.at[s], mix_in.at[me], m_send, m_recv.at[me], d).start()
        remote(stat_out.at[s], stat_in.at[me], s_send, s_recv.at[me], d).start()
        return carry

    lax.fori_loop(1, n, send_unit, 0)

    for d in range(1, n):
        remote(cand.at[peer(d)], cand.at[peer(d)], c_send, c_recv.at[peer(d)], d).wait_recv()
    values = [cand[s] for s in range(n)]

    def across(x, join):
        for f in range(1, fold):
            x = join(x, pltpu.roll(x, f * steps * reqs, 0))
        return x

    def folded(parts, join, reduce):
        x = functools.reduce(join, parts)
        pieces = [x[:, i * LANES : (i + 1) * LANES] for i in range(part // LANES)]
        x = reduce(functools.reduce(join, pieces), axis=1, keepdims=True)
        return across(jnp.broadcast_to(x, (crow, LANES)), join)

    def tile(x):
        return jnp.tile(x, (1, part // LANES))

    highest = folded(values, jnp.maximum, jnp.max)
    lowest = folded(
        [jnp.where(v > 0.5 * masked_value, v, -masked_value) for v in values], jnp.minimum, jnp.min
    )

    def search(_, state):
        low, high = state
        step = (high - low) * (1.0 / (PIVOTS + 1))
        pivots = [low + step * i for i in range(1, PIVOTS + 1)]
        new_low, new_high = low, high
        enough = []
        for pivot in pivots:
            wide_pivot = tile(pivot)
            count = folded(
                [jnp.where(v >= wide_pivot, 1.0, 0.0) for v in values], jnp.add, jnp.sum
            )
            enough.append(count >= picks)
        for pivot, yes in zip(pivots, enough):
            new_low = jnp.where(yes, pivot, new_low)
        for pivot, yes in reversed(list(zip(pivots, enough))):
            new_high = jnp.where(yes, new_high, pivot)
        return new_low, new_high

    low, _ = lax.fori_loop(0, ROUNDS, search, (lowest, highest))
    wide_low = tile(low)
    found = folded(
        [jnp.where(v >= wide_low, v, -masked_value) for v in values], jnp.minimum, jnp.min
    )
    column = found[:, :1]
    for t in range(steps):
        hit = iota((crow, reqs), 0) == t * reqs + iota((crow, reqs), 1)
        threshold_out[t : t + 1, :] = jnp.sum(jnp.where(hit, column, 0.0), axis=0, keepdims=True)

    for d in range(1, n):
        s = peer(d)
        remote(stat_in.at[s], stat_in.at[s], s_send, s_recv.at[s], d).wait_recv()
        remote(mix_in.at[s], mix_in.at[s], m_send, m_recv.at[s], d).wait_recv()
    peaks = [stat_in[s, 0:1, :] for s in range(n)]
    top = functools.reduce(jnp.maximum, peaks)
    shares = [stat_in[s, 1:2, :] * jnp.exp(peaks[s] - top) for s in range(n)]
    whole = functools.reduce(jnp.add, shares)
    held = jnp.int32(0)
    for r in range(reqs):
        held = held + jnp.where(owners[r] == me, 1, 0)
    keep = jnp.where(held > 0, 1.0, 0.0)
    merged = jnp.zeros((steps * heads, latent), jnp.float32)
    for s in range(n):
        merged = merged + mix_in[s].astype(jnp.float32) * to_column(shares[s] * keep / whole)
    result = merged.astype(jnp.bfloat16)
    for t in range(steps):
        attended_out[t, 0] = result[t * heads : (t + 1) * heads]

    for d in range(1, n):
        s = peer(d)
        remote(iq_all.at[me], iq_all.at[me], iq_send, iq_recv.at[me], d).wait_send()
        remote(q_all.at[me], q_all.at[me], q_send, q_recv.at[me], d).wait_send()
        remote(cand.at[me], cand.at[me], c_send, c_recv.at[me], d).wait_send()
        remote(mix_out.at[s], mix_in.at[me], m_send, m_recv.at[me], d).wait_send()
        remote(stat_out.at[s], stat_in.at[me], s_send, s_recv.at[me], d).wait_send()


def shards(
    cache, index_key, index_scale, lengths, owners, selected, query, index_query, index_weight
):
    n = lax.axis_size("seq")
    reqs, rows, width = cache.shape
    steps = selected.shape[0]
    heads = query.shape[2]
    iheads, idk = index_query.shape[2:]
    latent = width - ROPE
    fold = max(1, 8 // (steps * reqs))
    f32, bf16 = jnp.float32, jnp.bfloat16
    sems = [pltpu.SemaphoreType.DMA((2,))] + [pltpu.SemaphoreType.DMA((n,))] * 10
    vmem = pl.BlockSpec(memory_space=pltpu.VMEM)
    smem = pl.BlockSpec(memory_space=pltpu.SMEM)
    hbm = pl.BlockSpec(memory_space=pl.ANY)
    out = pl.pallas_call(
        functools.partial(kernel, n),
        out_shape=(
            jax.ShapeDtypeStruct((steps, reqs, rows), f32),
            jax.ShapeDtypeStruct((steps, reqs), f32),
            jax.ShapeDtypeStruct((steps, 1, heads, latent), bf16),
        ),
        in_specs=[smem, smem, hbm, hbm, vmem, vmem, vmem, vmem, vmem],
        out_specs=(vmem, vmem, vmem),
        scratch_shapes=[
            pltpu.VMEM((reqs, rows, width), bf16),
            pltpu.VMEM((reqs, rows, idk), bf16),
            pltpu.VMEM((n, steps * iheads + 16, idk), bf16),
            pltpu.VMEM((n, steps, heads, width), bf16),
            pltpu.VMEM((n, fold * steps * reqs, rows // fold), f32),
            pltpu.VMEM((reqs, steps, rows), f32),
            pltpu.VMEM((n, steps * heads, latent), bf16),
            pltpu.VMEM((n, 8, steps * heads), f32),
            pltpu.VMEM((n, steps * heads, latent), bf16),
            pltpu.VMEM((n, 8, steps * heads), f32),
        ]
        + sems,
        compiler_params=pltpu.CompilerParams(
            collective_id=0, has_side_effects=True, vmem_limit_bytes=40 * 2**20
        ),
    )(
        lengths, owners, cache, index_key, index_scale, selected, query, index_query, index_weight
    )
    return out


def solution(mesh):
    placed = (
        P(("groups", "req"), "seq", None),
        P(("groups", "req"), "seq", None),
        P(("groups", "req"), "seq"),
        P(("groups", "req")),
        P(("groups", "req")),
        P(None, ("groups", "req"), None),
        P(None, ("groups", "seq", "req"), "head", None),
        P(None, ("groups", "seq", "req"), None, None),
        P(None, ("groups", "seq", "req"), None),
    )
    return jax.shard_map(
        shards,
        mesh=mesh,
        in_specs=placed,
        out_specs=(
            P(None, ("groups", "req"), "seq"),
            P(None, ("groups", "req")),
            P(None, ("groups", "seq", "req"), "head", None),
        ),
        check_vma=False,
    )
```

time: 211 us -> 48.6 us (0.23)
  other arithmetic: 62.7 us -> 0 us
  blocking collectives: 57.5 us -> 0 us
  local copies, waits for them, and re-layouts: 66.4 us -> 10.7 us
  Pallas kernels: 0 us -> 36.8 us
  starting transfers between devices: 12.7 us -> 0 us
  matrix products: 5.34 us -> 0 us
  waiting for transfers between devices: 4.18 us -> 0 us
    all_gather x4 -> x0, blocking collectives: 57.5 us -> none  [the longest x1 19.6 us: shards(): all_queries = lax.all_gather(query, 'seq', axis=1, tiled=True)]
    top_k x3 -> x0, other arithmetic: 49.5 us -> none  [top_values(): return lax.top_k(jnp.concatenate([earlier, later], axis=-1), keep_count)[0]]
    pallas_call x0 -> x1, Pallas kernels: none -> 36.8 us  [shards(): pl.pallas_call(functools.partial(kernel, n), out_shape=(jax.ShapeDtypeStr...]
    unnamed x26 -> x21, local copies, waits for them, and re-layouts: 40.3 us -> 10.7 us
    gather x5 -> x0, local copies, waits for them, and re-layouts: 24.3 us -> none  [the longest x2 22.6 us: shards(): jnp.take(flat_cache, request_ids[None, :, None] * shard_rows + slot_posit...]
    all_to_all x3 -> x0, starting transfers between devices: 12.7 us -> none  [the longest x1 5.61 us: shards(): lax.all_to_all(outbound[0], 'seq', split_axis=1, concat_axis=1, tiled=True)]
    dot_general x6 -> x0, matrix products: 5.34 us -> none  [the longest x1 2.98 us: shards(): jnp.einsum('tjhc,tjcd->tjhd', weights.astype(jnp.bfloat16), local_rows, p...]
    all_to_all x3 -> x0, waiting for transfers between devices: 4.18 us -> none  [the longest x1 4.17 us: shards(): lax.all_to_all(outbound[2], 'seq', split_axis=1, concat_axis=1, tiled=True)]
  transfers between devices with their start and end apart: 3 -> 0, of which waited for: 1 -> 0; matrix products, arithmetic and copies ran while one was open for 29% -> 0% of each run, Pallas kernels for 0% -> 0%
where the time goes in v1:
time: 48.6 us; the launch traced here: 48.3 us
  Pallas kernels  36.8 us (76%)
  local copies, waits for them, and re-layouts  10.7 us (22%)
  between operations  0.74 us (2%)
    pallas_call x1, Pallas kernels, shards(): pl.pallas_call(functools.partial(kernel, n), out_shape=(jax.ShapeDtypeStr...  36.8 us
    unnamed x21, local copies, waits for them, and re-layouts  10.7 us

profile of v1, /device:TPU:0, one launch (start us, length us, event | category | flops | bytes accessed | tf_op | source)
XLA Modules:
  0.0 48.3 jit_solution(10715913890868565967)
XLA Ops:
  0.6 0.0 copy-start.4
  0.6 0.0 copy-start.2
  0.7 0.0 copy-start.3
  0.7 0.0 copy-start.7
  0.7 0.0 copy-start.6
  0.7 0.0 copy-start.5
  0.7 0.0 copy-start.1
  0.7 0.8 %copy.13.iw_ref = bf16[2,1,64]{2,1,0:T(2,128)(2,1)S(1)} copy(bf16[2,1,64]{2,0,1:T(2,128)(2,1)} %param.17) | data formatting | bytes 512 | tf_op args[8]
  1.5 6.0 %copy.12.cache_hbm = bf16[2,1536,576]{2,1,0:T(8,128)(2,1)} copy(bf16[2,1536,576]{1,2,0:T(8,128)(2,1)} %param.9) | data formatting | bytes 7077888 | tf_op args[0]
  7.4 0.0 copy-done.4
  7.4 0.0 copy-done.2
  7.4 0.0 copy-done.3
  7.4 0.0 copy-done.7
  7.4 0.0 copy-done.6
  7.4 0.0 copy-done.5
  7.5 0.0 copy-done.1
  7.5 0.0 copy-start
  7.5 2.1 %copy-done = bf16[2,1536,576]{2,1,0:T(8,128)(2,1)S(1)} copy-done((bf16[2,1536,576]{2,1,0:T(8,128)(2,1)S(1)}, bf16[2,1536,576]{2,1,0:T(8,128)(2,1)}, u32[]{:S(2)}) %copy-start) | copy-done | bytes 3538968
  9.6 36.8 %shard_map.112 = (f32[2,2,1536]{2,1,0:T(2,128)S(1)}, f32[2,2]{1,0:T(2,128)S(1)}, bf16[2,1,64,512]{3,2,1,0:T(8,128)(2,1)S(1)}) custom-call(s32[2]{0:T(128)S(1)} %copy-done.6, s32[2]{0:T(128)S(1)} %copy-done.7, bf16[2,1536,576]{2,1,0:T(8,128)(2,1)S(1)} %copy-done, bf16[2,1536,128]{2,1,0:T(8,128)(2,1)S(1)} %copy-done.1, f32[2,1536]{1,0:T(2,128)S(1)} %copy-done.5, ...), custom_call_target="tpu_custom_call" | custom-call | tf_op jit(solution)/shard_map/pallas_call | solution.py:286
  46.4 0.6 %copy.17 = f32[2,2,1536]{2,1,0:T(2,128)} copy(f32[2,2,1536]{2,1,0:T(2,128)S(1)} %get-tuple-element.6) | data formatting | bytes 49152
  47.0 0.6 %copy.18 = f32[2,2]{1,0:T(2,128)} copy(f32[2,2]{1,0:T(2,128)S(1)} %get-tuple-element.7) | data formatting | bytes 32
  47.6 0.7 %copy.19 = bf16[2,1,64,512]{3,2,1,0:T(8,128)(2,1)} copy(bf16[2,1,64,512]{3,2,1,0:T(8,128)(2,1)S(1)} %get-tuple-element.8) | data formatting | bytes 262144
Async XLA Ops:
  0.6 6.8 %copy-start.4 = (bf16[2,1,64,128]{3,2,1,0:T(8,128)(2,1)S(1)}, bf16[2,1,64,128]{3,2,1,0:T(8,128)(2,1)}, u32[]{:S(2)}) copy-start(bf16[2,1,64,128]{3,2,1,0:T(8,128)(2,1)} %iq_ref.1) | copy-start | bytes 98308
  0.6 6.8 %copy-start.2 = (bf16[2,1,64,576]{3,2,1,0:T(8,128)(2,1)S(1)}, bf16[2,1,64,576]{3,2,1,0:T(8,128)(2,1)}, u32[]{:S(2)}) copy-start(bf16[2,1,64,576]{3,2,1,0:T(8,128)(2,1)} %query_ref.1) | copy-start | bytes 442372
  0.7 6.8 %copy-start.3 = (s32[2,2,2048]{2,1,0:T(2,128)S(1)}, s32[2,2,2048]{2,1,0:T(2,128)}, u32[]{:S(2)}) copy-start(s32[2,2,2048]{2,1,0:T(2,128)} %selected_ref.1) | copy-start | bytes 98308
  0.7 6.8 %copy-start.7 = (s32[2]{0:T(128)S(1)}, s32[2]{0:T(128)}, u32[]{:S(2)}) copy-start(s32[2]{0:T(128)} %owners.1) | copy-start | bytes 28
  0.7 6.8 %copy-start.6 = (s32[2]{0:T(128)S(1)}, s32[2]{0:T(128)}, u32[]{:S(2)}) copy-start(s32[2]{0:T(128)} %lengths.1) | copy-start | bytes 28
  0.7 6.8 %copy-start.5 = (f32[2,1536]{1,0:T(2,128)S(1)}, f32[2,1536]{1,0:T(2,128)}, u32[]{:S(2)}) copy-start(f32[2,1536]{1,0:T(2,128)} %scale_ref.1) | copy-start | bytes 36868
  0.7 6.8 %copy-start.1 = (bf16[2,1536,128]{2,1,0:T(8,128)(2,1)S(1)}, bf16[2,1536,128]{2,1,0:T(8,128)(2,1)}, u32[]{:S(2)}) copy-start(bf16[2,1536,128]{2,1,0:T(8,128)(2,1)} %key_hbm.1) | copy-start | bytes 2359300
  7.5 2.1 %copy-start = (bf16[2,1536,576]{2,1,0:T(8,128)(2,1)S(1)}, bf16[2,1536,576]{2,1,0:T(8,128)(2,1)}, u32[]{:S(2)}) copy-start(bf16[2,1536,576]{2,1,0:T(8,128)(2,1)} %copy.12.cache_hbm) | copy-start | bytes 10616836

commit v2 on v1

--- a/solution.py
+++ b/solution.py
@@ -76,7 +76,7 @@
 ):
     me = lax.axis_index("seq")
     steps, reqs, picks = selected_ref.shape
-    rows = cache_v.shape[1]
+    rows = cache_v.shape[2]
     heads = query_ref.shape[2]
     latent = mix_in.shape[2]
     iheads = iq_ref.shape[2]
@@ -108,7 +108,7 @@
         )
     for t in range(steps):
         iq_all[me, t * iheads : (t + 1) * iheads, :] = iq_ref[t, 0]
-    wide = jnp.concatenate([iw_ref[t] for t in range(steps)], axis=0).astype(jnp.float32)
+    wide = iw_ref[...].astype(jnp.float32)
     iq_all[me, steps * iheads :, :] = jnp.pad(
         wide, ((0, 16 - steps), (0, LANES - iheads))
     ).astype(jnp.bfloat16)
@@ -139,6 +139,7 @@
         remote(iq_all.at[peer(d)], iq_all.at[peer(d)], iq_send, iq_recv.at[peer(d)], d).wait_recv()
     position = base + iota((1, rows), 1)
     part = rows // fold
+    pieces = {}
     for j in range(reqs):
         packed = iq_all[owners[j]]
         dots = jnp.maximum(dot(packed[: steps * iheads], key_v[j], NT), 0.0)
@@ -153,8 +154,9 @@
             scores_out[t, j : j + 1, :] = jnp.where(inside, total, 0.0)
             candidates = jnp.where(inside, total, masked_value)
             for f in range(fold):
-                at = f * steps * reqs + t * reqs + j
-                cand[me, at : at + 1, :] = candidates[:, f * part : (f + 1) * part]
+                pieces[f * steps * reqs + t * reqs + j] = candidates[:, f * part : (f + 1) * part]
+    ordered = [pieces[i] for i in range(crow)]
+    cand[me] = jnp.concatenate(ordered, axis=0).astype(jnp.bfloat16)
     for d in range(1, n):
         remote(cand.at[me], cand.at[me], c_send, c_recv.at[me], d).start()
 
@@ -165,7 +167,7 @@
         for r in range(reqs):
             j = j + jnp.where(owners[r] == s, r, 0)
         latents = cache_v[j]
-        logits = dot(q_all[s].reshape(steps * heads, -1), latents, NT) * score_scale
+        logits = dot(q_all[s].reshape(steps * heads, -1), latents, NN) * score_scale
         mask = bias[j]
         logits = jnp.concatenate(
             [logits[t * heads : (t + 1) * heads] + mask[t : t + 1] for t in range(steps)], axis=0
@@ -173,7 +175,7 @@
         peak = jnp.max(logits, axis=1, keepdims=True)
         weights = jnp.exp(logits - peak)
         total = jnp.sum(weights, axis=1, keepdims=True)
-        mixture = dot(weights.astype(jnp.bfloat16), latents[:, :latent], NN) / total
+        mixture = dot(weights.astype(jnp.bfloat16), latents[:latent], NT) / total
         stat = jnp.concatenate([to_row(peak), to_row(total)], axis=0)
         return mixture.astype(jnp.bfloat16), jnp.pad(stat, ((0, 6), (0, 0)))
 
@@ -191,11 +193,12 @@
 
     for d in range(1, n):
         remote(cand.at[peer(d)], cand.at[peer(d)], c_send, c_recv.at[peer(d)], d).wait_recv()
-    values = [cand[s] for s in range(n)]
+    values = [cand[s].astype(jnp.float32) for s in range(n)]
 
     def across(x, join):
+        own = x
         for f in range(1, fold):
-            x = join(x, pltpu.roll(x, f * steps * reqs, 0))
+            x = join(x, pltpu.roll(own, f * steps * reqs, 0))
         return x
 
     def folded(parts, join, reduce):
@@ -277,7 +280,7 @@
     heads = query.shape[2]
     iheads, idk = index_query.shape[2:]
     latent = width - ROPE
-    fold = max(1, 8 // (steps * reqs))
+    fold = max(1, 16 // (steps * reqs))
     f32, bf16 = jnp.float32, jnp.bfloat16
     sems = [pltpu.SemaphoreType.DMA((2,))] + [pltpu.SemaphoreType.DMA((n,))] * 10
     vmem = pl.BlockSpec(memory_space=pltpu.VMEM)
@@ -293,11 +296,11 @@
         in_specs=[smem, smem, hbm, hbm, vmem, vmem, vmem, vmem, vmem],
         out_specs=(vmem, vmem, vmem),
         scratch_shapes=[
-            pltpu.VMEM((reqs, rows, width), bf16),
+            pltpu.VMEM((reqs, width, rows), bf16),
             pltpu.VMEM((reqs, rows, idk), bf16),
             pltpu.VMEM((n, steps * iheads + 16, idk), bf16),
             pltpu.VMEM((n, steps, heads, width), bf16),
-            pltpu.VMEM((n, fold * steps * reqs, rows // fold), f32),
+            pltpu.VMEM((n, fold * steps * reqs, rows // fold), bf16),
             pltpu.VMEM((reqs, steps, rows), f32),
             pltpu.VMEM((n, steps * heads, latent), bf16),
             pltpu.VMEM((n, 8, steps * heads), f32),
@@ -306,10 +309,18 @@
         ]
         + sems,
         compiler_params=pltpu.CompilerParams(
-            collective_id=0, has_side_effects=True, vmem_limit_bytes=40 * 2**20
+            collective_id=0, has_side_effects=True, vmem_limit_bytes=60 * 2**20
         ),
     )(
-        lengths, owners, cache, index_key, index_scale, selected, query, index_query, index_weight
+        lengths,
+        owners,
+        jnp.swapaxes(cache, 1, 2),
+        index_key,
+        index_scale,
+        selected,
+        query,
+        index_query,
+        index_weight[:, 0],
     )
     return out
 

time: 48.6 us -> 41.9 us (0.86)
  the two profiles are of different devices: /device:TPU:0 before, /device:TPU:22 now
where the time goes in v2:
time: 41.9 us; the launch traced here: 41.6 us
  Pallas kernels  36.9 us (88%)
  local copies, waits for them, and re-layouts  4.11 us (10%)
  between operations  0.64 us (2%)
    pallas_call x1, Pallas kernels, shards(): pl.pallas_call(functools.partial(kernel, n), out_shape=(jax.ShapeDtypeStr...  36.9 us
    unnamed x3, local copies, waits for them, and re-layouts  4.11 us

profile of v2, /device:TPU:22, one launch (start us, length us, event | category | flops | bytes accessed | tf_op | source)
XLA Modules:
  0.0 41.6 jit_solution(4447540756323442991)
XLA Ops:
  0.6 36.9 %shard_map.112 = (f32[2,2,1536]{2,1,0:T(2,128)}, f32[2,2]{1,0:T(2,128)}, bf16[2,1,64,512]{3,2,1,0:T(8,128)(2,1)}) custom-call(s32[2]{0:T(128)} %lengths.1, s32[2]{0:T(128)} %owners.1, bf16[2,576,1536]{2,1,0:T(8,128)(2,1)} %bitcast.2, bf16[2,1536,128]{2,1,0:T(8,128)(2,1)} %key_hbm.1, f32[2,1536]{1,0:T(2,128)} %scale_ref.1, s32[2,2,2048]{2,1,0:T(2,128)} %selected_ref.1, ...), custom_call_target="tpu_custom_call" | custom-call | tf_op jit(solution)/shard_map/pallas_call | solution.py:289
  37.5 1.3 %copy.15 = f32[2,2,1536]{2,1,0:T(2,128)} copy(f32[2,2,1536]{2,1,0:T(2,128)} %get-tuple-element.6) | data formatting | bytes 49152
  38.9 1.2 %copy.16 = f32[2,2]{1,0:T(2,128)} copy(f32[2,2]{1,0:T(2,128)} %get-tuple-element.7) | data formatting | bytes 32
  40.1 1.6 %copy.17 = bf16[2,1,64,512]{3,2,1,0:T(8,128)(2,1)} copy(bf16[2,1,64,512]{3,2,1,0:T(8,128)(2,1)} %get-tuple-element.8) | data formatting | bytes 262144

commit v3 on v2

--- a/solution.py
+++ b/solution.py
@@ -66,6 +66,7 @@
     iq_send,
     iq_recv,
     q_send,
+    q_left,
     q_recv,
     c_send,
     c_recv,
@@ -117,8 +118,23 @@
 
     for d in range(1, n):
         remote(iq_all.at[me], iq_all.at[me], iq_send, iq_recv.at[me], d).start()
-    for d in range(1, n):
-        remote(q_all.at[me], q_all.at[me], q_send, q_recv.at[me], d).start()
+    def hop(shard, to, send):
+        return pltpu.make_async_remote_copy(
+            src_ref=q_all.at[shard],
+            dst_ref=q_all.at[shard],
+            send_sem=send.at[shard],
+            recv_sem=q_recv.at[shard],
+            device_id={"seq": to},
+            device_id_type=pl.DeviceIdType.MESH,
+        )
+
+    @pl.when(me < n - 1)
+    def _():
+        hop(me, me + 1, q_send).start()
+
+    @pl.when(me > 0)
+    def _():
+        hop(me, me - 1, q_left).start()
 
     base = me * rows
     blocks = rows // LANES
@@ -181,15 +197,41 @@
 
     mix_in[me], stat_in[me] = unit(me)
 
-    def send_unit(d, carry):
-        s = peer(d)
-        remote(q_all.at[s], q_all.at[s], q_send, q_recv.at[s], d).wait_recv()
+    def send_unit(s, d):
         mix_out[s], stat_out[s] = unit(s)
         remote(mix_out.at[s], mix_in.at[me], m_send, m_recv.at[me], d).start()
         remote(stat_out.at[s], stat_in.at[me], s_send, s_recv.at[me], d).start()
+
+    def distance(d, carry):
+        below, above = me - d, me + d
+
+        @pl.when(below >= 0)
+        def _():
+            hop(below, below, q_send).wait_recv()
+
+            @pl.when(me < n - 1)
+            def _():
+                hop(below, me + 1, q_send).start()
+
+        @pl.when(above < n)
+        def _():
+            hop(above, above, q_left).wait_recv()
+
+            @pl.when(me > 0)
+            def _():
+                hop(above, me - 1, q_left).start()
+
+        @pl.when(below >= 0)
+        def _():
+            send_unit(below, n - d)
+
+        @pl.when(above < n)
+        def _():
+            send_unit(above, d)
+
         return carry
 
-    lax.fori_loop(1, n, send_unit, 0)
+    lax.fori_loop(1, n, distance, 0)
 
     for d in range(1, n):
         remote(cand.at[peer(d)], cand.at[peer(d)], c_send, c_recv.at[peer(d)], d).wait_recv()
@@ -265,10 +307,18 @@
     for d in range(1, n):
         s = peer(d)
         remote(iq_all.at[me], iq_all.at[me], iq_send, iq_recv.at[me], d).wait_send()
-        remote(q_all.at[me], q_all.at[me], q_send, q_recv.at[me], d).wait_send()
         remote(cand.at[me], cand.at[me], c_send, c_recv.at[me], d).wait_send()
         remote(mix_out.at[s], mix_in.at[me], m_send, m_recv.at[me], d).wait_send()
         remote(stat_out.at[s], stat_in.at[me], s_send, s_recv.at[me], d).wait_send()
+    for d in range(n - 1):
+
+        @pl.when((me - d >= 0) & (me < n - 1))
+        def _():
+            hop(me - d, me + 1, q_send).wait_send()
+
+        @pl.when((me + d < n) & (me > 0))
+        def _():
+            hop(me + d, me - 1, q_left).wait_send()
 
 
 def shards(
@@ -282,7 +332,7 @@
     latent = width - ROPE
     fold = max(1, 16 // (steps * reqs))
     f32, bf16 = jnp.float32, jnp.bfloat16
-    sems = [pltpu.SemaphoreType.DMA((2,))] + [pltpu.SemaphoreType.DMA((n,))] * 10
+    sems = [pltpu.SemaphoreType.DMA((2,))] + [pltpu.SemaphoreType.DMA((n,))] * 11
     vmem = pl.BlockSpec(memory_space=pltpu.VMEM)
     smem = pl.BlockSpec(memory_space=pltpu.SMEM)
     hbm = pl.BlockSpec(memory_space=pl.ANY)
@@ -309,7 +359,7 @@
         ]
         + sems,
         compiler_params=pltpu.CompilerParams(
-            collective_id=0, has_side_effects=True, vmem_limit_bytes=60 * 2**20
+            collective_id=0, has_side_effects=True, vmem_limit_bytes=53 * 2**20
         ),
     )(
         lengths,

time: 41.9 us -> 42 us (level)
  the two profiles are of different devices: /device:TPU:22 before, /device:TPU:0 now
where the time goes in v3:
time: 42 us; the launch traced here: 41.6 us
  Pallas kernels  34.1 us (81%)
  local copies, waits for them, and re-layouts  6.92 us (16%)
  between operations  0.66 us (2%)
    pallas_call x1, Pallas kernels, shards(): pl.pallas_call(functools.partial(kernel, n), out_shape=(jax.ShapeDtypeStr...  34.1 us
    unnamed x17, local copies, waits for them, and re-layouts  6.92 us

profile of v3, /device:TPU:0, one launch (start us, length us, event | category | flops | bytes accessed | tf_op | source)
XLA Modules:
  0.0 41.6 jit_solution(2549902107368915098)
XLA Ops:
  0.6 0.0 copy-start
  0.6 0.9 %copy-done = bf16[2,1,64,576]{3,2,1,0:T(8,128)(2,1)S(1)} copy-done((bf16[2,1,64,576]{3,2,1,0:T(8,128)(2,1)S(1)}, bf16[2,1,64,576]{3,2,1,0:T(8,128)(2,1)}, u32[]{:S(2)}) %copy-start) | copy-done | bytes 147480
  1.6 0.0 copy-start.1
  1.6 0.8 %copy-done.1 = s32[2,2,2048]{2,1,0:T(2,128)S(1)} copy-done((s32[2,2,2048]{2,1,0:T(2,128)S(1)}, s32[2,2,2048]{2,1,0:T(2,128)}, u32[]{:S(2)}) %copy-start.1) | copy-done | bytes 32792
  2.3 0.0 copy-start.2
  2.3 0.8 %copy-done.2 = bf16[2,1,64,128]{3,2,1,0:T(8,128)(2,1)S(1)} copy-done((bf16[2,1,64,128]{3,2,1,0:T(8,128)(2,1)S(1)}, bf16[2,1,64,128]{3,2,1,0:T(8,128)(2,1)}, u32[]{:S(2)}) %copy-start.2) | copy-done | bytes 32792
  3.1 0.0 copy-start.3
  3.1 0.7 %copy-done.3 = f32[2,1536]{1,0:T(2,128)S(1)} copy-done((f32[2,1536]{1,0:T(2,128)S(1)}, f32[2,1536]{1,0:T(2,128)}, u32[]{:S(2)}) %copy-start.3) | copy-done | bytes 12312
  3.8 0.0 copy-start.4
  3.8 0.7 %copy-done.4 = s32[2]{0:T(128)S(1)} copy-done((s32[2]{0:T(128)S(1)}, s32[2]{0:T(128)}, u32[]{:S(2)}) %copy-start.4) | copy-done | bytes 32
  4.4 0.0 copy-start.5
  4.4 0.7 %copy-done.5 = s32[2]{0:T(128)S(1)} copy-done((s32[2]{0:T(128)S(1)}, s32[2]{0:T(128)}, u32[]{:S(2)}) %copy-start.5) | copy-done | bytes 32
  5.1 0.0 copy-start.6
  5.1 0.7 %copy-done.6 = bf16[2,1,64]{2,0,1:T(2,128)(2,1)S(1)} copy-done((bf16[2,1,64]{2,0,1:T(2,128)(2,1)S(1)}, bf16[2,1,64]{2,0,1:T(2,128)(2,1)}, u32[]{:S(2)}) %copy-start.6) | copy-done | bytes 280
  5.7 34.1 %shard_map.112 = (f32[2,2,1536]{2,1,0:T(2,128)S(1)}, f32[2,2]{1,0:T(2,128)S(1)}, bf16[2,1,64,512]{3,2,1,0:T(8,128)(2,1)S(1)}) custom-call(s32[2]{0:T(128)S(1)} %copy-done.4, s32[2]{0:T(128)S(1)} %copy-done.5, bf16[2,576,1536]{2,1,0:T(8,128)(2,1)} %bitcast.3, bf16[2,1536,128]{2,1,0:T(8,128)(2,1)} %key_hbm.1, f32[2,1536]{1,0:T(2,128)S(1)} %copy-done.3, ...), custom_call_target="tpu_custom_call" | custom-call | tf_op jit(solution)/shard_map/pallas_call | solution.py:339
  39.8 0.6 %copy.15 = f32[2,2,1536]{2,1,0:T(2,128)} copy(f32[2,2,1536]{2,1,0:T(2,128)S(1)} %get-tuple-element.6) | data formatting | bytes 49152
  40.4 0.6 %copy.16 = f32[2,2]{1,0:T(2,128)} copy(f32[2,2]{1,0:T(2,128)S(1)} %get-tuple-element.7) | data formatting | bytes 32
  41.0 0.7 %copy.17 = bf16[2,1,64,512]{3,2,1,0:T(8,128)(2,1)} copy(bf16[2,1,64,512]{3,2,1,0:T(8,128)(2,1)S(1)} %get-tuple-element.8) | data formatting | bytes 262144
Async XLA Ops:
  0.6 0.9 %copy-start = (bf16[2,1,64,576]{3,2,1,0:T(8,128)(2,1)S(1)}, bf16[2,1,64,576]{3,2,1,0:T(8,128)(2,1)}, u32[]{:S(2)}) copy-start(bf16[2,1,64,576]{3,2,1,0:T(8,128)(2,1)} %query_ref.1) | copy-start | bytes 442372
  1.6 0.8 %copy-start.1 = (s32[2,2,2048]{2,1,0:T(2,128)S(1)}, s32[2,2,2048]{2,1,0:T(2,128)}, u32[]{:S(2)}) copy-start(s32[2,2,2048]{2,1,0:T(2,128)} %selected_ref.1) | copy-start | bytes 98308
  2.3 0.8 %copy-start.2 = (bf16[2,1,64,128]{3,2,1,0:T(8,128)(2,1)S(1)}, bf16[2,1,64,128]{3,2,1,0:T(8,128)(2,1)}, u32[]{:S(2)}) copy-start(bf16[2,1,64,128]{3,2,1,0:T(8,128)(2,1)} %iq_ref.1) | copy-start | bytes 98308
  3.1 0.7 %copy-start.3 = (f32[2,1536]{1,0:T(2,128)S(1)}, f32[2,1536]{1,0:T(2,128)}, u32[]{:S(2)}) copy-start(f32[2,1536]{1,0:T(2,128)} %scale_ref.1) | copy-start | bytes 36868
  3.8 0.7 %copy-start.4 = (s32[2]{0:T(128)S(1)}, s32[2]{0:T(128)}, u32[]{:S(2)}) copy-start(s32[2]{0:T(128)} %lengths.1) | copy-start | bytes 28
  4.4 0.7 %copy-start.5 = (s32[2]{0:T(128)S(1)}, s32[2]{0:T(128)}, u32[]{:S(2)}) copy-start(s32[2]{0:T(128)} %owners.1) | copy-start | bytes 28
  5.1 0.7 %copy-start.6 = (bf16[2,1,64]{2,0,1:T(2,128)(2,1)S(1)}, bf16[2,1,64]{2,0,1:T(2,128)(2,1)}, u32[]{:S(2)}) copy-start(bf16[2,1,64]{2,0,1:T(2,128)(2,1)} %param.17) | copy-start | bytes 772

commit v4 on v2

--- a/solution.py
+++ b/solution.py
@@ -309,7 +309,7 @@
         ]
         + sems,
         compiler_params=pltpu.CompilerParams(
-            collective_id=0, has_side_effects=True, vmem_limit_bytes=60 * 2**20
+            collective_id=0, has_side_effects=True, vmem_limit_bytes=53 * 2**20
         ),
     )(
         lengths,

time: 41.9 us -> 43.7 us (1.043)
  the two profiles are of different devices: /device:TPU:22 before, /device:TPU:16 now
where the time goes in v4:
time: 43.7 us; the launch traced here: 43.3 us
  Pallas kernels  35.7 us (82%)
  local copies, waits for them, and re-layouts  6.92 us (16%)
  between operations  0.66 us (2%)
    pallas_call x1, Pallas kernels, shards(): pl.pallas_call(functools.partial(kernel, n), out_shape=(jax.ShapeDtypeStr...  35.7 us
    unnamed x17, local copies, waits for them, and re-layouts  6.92 us

profile of v4, /device:TPU:16, one launch (start us, length us, event | category | flops | bytes accessed | tf_op | source)
XLA Modules:
  0.0 43.3 jit_solution(11480370831813169264)
XLA Ops:
  0.6 0.0 copy-start
  0.6 0.9 %copy-done = bf16[2,1,64,576]{3,2,1,0:T(8,128)(2,1)S(1)} copy-done((bf16[2,1,64,576]{3,2,1,0:T(8,128)(2,1)S(1)}, bf16[2,1,64,576]{3,2,1,0:T(8,128)(2,1)}, u32[]{:S(2)}) %copy-start) | copy-done | bytes 147480
  1.6 0.0 copy-start.1
  1.6 0.8 %copy-done.1 = s32[2,2,2048]{2,1,0:T(2,128)S(1)} copy-done((s32[2,2,2048]{2,1,0:T(2,128)S(1)}, s32[2,2,2048]{2,1,0:T(2,128)}, u32[]{:S(2)}) %copy-start.1) | copy-done | bytes 32792
  2.3 0.0 copy-start.2
  2.3 0.8 %copy-done.2 = bf16[2,1,64,128]{3,2,1,0:T(8,128)(2,1)S(1)} copy-done((bf16[2,1,64,128]{3,2,1,0:T(8,128)(2,1)S(1)}, bf16[2,1,64,128]{3,2,1,0:T(8,128)(2,1)}, u32[]{:S(2)}) %copy-start.2) | copy-done | bytes 32792
  3.1 0.0 copy-start.3
  3.1 0.7 %copy-done.3 = f32[2,1536]{1,0:T(2,128)S(1)} copy-done((f32[2,1536]{1,0:T(2,128)S(1)}, f32[2,1536]{1,0:T(2,128)}, u32[]{:S(2)}) %copy-start.3) | copy-done | bytes 12312
  3.8 0.0 copy-start.4
  3.8 0.7 %copy-done.4 = s32[2]{0:T(128)S(1)} copy-done((s32[2]{0:T(128)S(1)}, s32[2]{0:T(128)}, u32[]{:S(2)}) %copy-start.4) | copy-done | bytes 32
  4.4 0.0 copy-start.5
  4.4 0.7 %copy-done.5 = s32[2]{0:T(128)S(1)} copy-done((s32[2]{0:T(128)S(1)}, s32[2]{0:T(128)}, u32[]{:S(2)}) %copy-start.5) | copy-done | bytes 32
  5.1 0.0 copy-start.6
  5.1 0.7 %copy-done.6 = bf16[2,1,64]{2,0,1:T(2,128)(2,1)S(1)} copy-done((bf16[2,1,64]{2,0,1:T(2,128)(2,1)S(1)}, bf16[2,1,64]{2,0,1:T(2,128)(2,1)}, u32[]{:S(2)}) %copy-start.6) | copy-done | bytes 280
  5.7 35.7 %shard_map.112 = (f32[2,2,1536]{2,1,0:T(2,128)S(1)}, f32[2,2]{1,0:T(2,128)S(1)}, bf16[2,1,64,512]{3,2,1,0:T(8,128)(2,1)S(1)}) custom-call(s32[2]{0:T(128)S(1)} %copy-done.4, s32[2]{0:T(128)S(1)} %copy-done.5, bf16[2,576,1536]{2,1,0:T(8,128)(2,1)} %bitcast.3, bf16[2,1536,128]{2,1,0:T(8,128)(2,1)} %key_hbm.1, f32[2,1536]{1,0:T(2,128)S(1)} %copy-done.3, ...), custom_call_target="tpu_custom_call" | custom-call | tf_op jit(solution)/shard_map/pallas_call | solution.py:289
  41.5 0.6 %copy.15 = f32[2,2,1536]{2,1,0:T(2,128)} copy(f32[2,2,1536]{2,1,0:T(2,128)S(1)} %get-tuple-element.6) | data formatting | bytes 49152
  42.1 0.6 %copy.16 = f32[2,2]{1,0:T(2,128)} copy(f32[2,2]{1,0:T(2,128)S(1)} %get-tuple-element.7) | data formatting | bytes 32
  42.7 0.7 %copy.17 = bf16[2,1,64,512]{3,2,1,0:T(8,128)(2,1)} copy(bf16[2,1,64,512]{3,2,1,0:T(8,128)(2,1)S(1)} %get-tuple-element.8) | data formatting | bytes 262144
Async XLA Ops:
  0.6 0.9 %copy-start = (bf16[2,1,64,576]{3,2,1,0:T(8,128)(2,1)S(1)}, bf16[2,1,64,576]{3,2,1,0:T(8,128)(2,1)}, u32[]{:S(2)}) copy-start(bf16[2,1,64,576]{3,2,1,0:T(8,128)(2,1)} %query_ref.1) | copy-start | bytes 442372
  1.6 0.8 %copy-start.1 = (s32[2,2,2048]{2,1,0:T(2,128)S(1)}, s32[2,2,2048]{2,1,0:T(2,128)}, u32[]{:S(2)}) copy-start(s32[2,2,2048]{2,1,0:T(2,128)} %selected_ref.1) | copy-start | bytes 98308
  2.3 0.8 %copy-start.2 = (bf16[2,1,64,128]{3,2,1,0:T(8,128)(2,1)S(1)}, bf16[2,1,64,128]{3,2,1,0:T(8,128)(2,1)}, u32[]{:S(2)}) copy-start(bf16[2,1,64,128]{3,2,1,0:T(8,128)(2,1)} %iq_ref.1) | copy-start | bytes 98308
  3.1 0.7 %copy-start.3 = (f32[2,1536]{1,0:T(2,128)S(1)}, f32[2,1536]{1,0:T(2,128)}, u32[]{:S(2)}) copy-start(f32[2,1536]{1,0:T(2,128)} %scale_ref.1) | copy-start | bytes 36868
  3.8 0.7 %copy-start.4 = (s32[2]{0:T(128)S(1)}, s32[2]{0:T(128)}, u32[]{:S(2)}) copy-start(s32[2]{0:T(128)} %lengths.1) | copy-start | bytes 28
  4.4 0.7 %copy-start.5 = (s32[2]{0:T(128)S(1)}, s32[2]{0:T(128)}, u32[]{:S(2)}) copy-start(s32[2]{0:T(128)} %owners.1) | copy-start | bytes 28
  5.1 0.7 %copy-start.6 = (bf16[2,1,64]{2,0,1:T(2,128)(2,1)S(1)}, bf16[2,1,64]{2,0,1:T(2,128)(2,1)}, u32[]{:S(2)}) copy-start(bf16[2,1,64]{2,0,1:T(2,128)(2,1)} %param.17) | copy-start | bytes 772

commit v5 on v3

--- a/solution.py
+++ b/solution.py
@@ -359,7 +359,7 @@
         ]
         + sems,
         compiler_params=pltpu.CompilerParams(
-            collective_id=0, has_side_effects=True, vmem_limit_bytes=53 * 2**20
+            collective_id=0, has_side_effects=True, vmem_limit_bytes=60 * 2**20
         ),
     )(
         lengths,

time: 42 us -> 40.2 us (0.957)
  local copies, waits for them, and re-layouts: 6.92 us -> 4.11 us
  Pallas kernels: 34.1 us -> 35.2 us
    unnamed x17 -> x3, local copies, waits for them, and re-layouts: 6.92 us -> 4.11 us
    pallas_call x1, Pallas kernels: 34.1 us -> 35.2 us  [shards(): pl.pallas_call(functools.partial(kernel, n), out_shape=(jax.ShapeDtypeStr...]
where the time goes in v5:
time: 40.2 us; the launch traced here: 40 us
  Pallas kernels  35.2 us (88%)
  local copies, waits for them, and re-layouts  4.11 us (10%)
  between operations  0.64 us (2%)
    pallas_call x1, Pallas kernels, shards(): pl.pallas_call(functools.partial(kernel, n), out_shape=(jax.ShapeDtypeStr...  35.2 us
    unnamed x3, local copies, waits for them, and re-layouts  4.11 us

profile of v5, /device:TPU:0, one launch (start us, length us, event | category | flops | bytes accessed | tf_op | source)
XLA Modules:
  0.0 40.0 jit_solution(11103972182282633827)
XLA Ops:
  0.6 35.2 %shard_map.112 = (f32[2,2,1536]{2,1,0:T(2,128)}, f32[2,2]{1,0:T(2,128)}, bf16[2,1,64,512]{3,2,1,0:T(8,128)(2,1)}) custom-call(s32[2]{0:T(128)} %lengths.1, s32[2]{0:T(128)} %owners.1, bf16[2,576,1536]{2,1,0:T(8,128)(2,1)} %bitcast.2, bf16[2,1536,128]{2,1,0:T(8,128)(2,1)} %key_hbm.1, f32[2,1536]{1,0:T(2,128)} %scale_ref.1, s32[2,2,2048]{2,1,0:T(2,128)} %selected_ref.1, ...), custom_call_target="tpu_custom_call" | custom-call | tf_op jit(solution)/shard_map/pallas_call | solution.py:339
  35.8 1.3 %copy.15 = f32[2,2,1536]{2,1,0:T(2,128)} copy(f32[2,2,1536]{2,1,0:T(2,128)} %get-tuple-element.6) | data formatting | bytes 49152
  37.2 1.2 %copy.16 = f32[2,2]{1,0:T(2,128)} copy(f32[2,2]{1,0:T(2,128)} %get-tuple-element.7) | data formatting | bytes 32
  38.4 1.6 %copy.17 = bf16[2,1,64,512]{3,2,1,0:T(8,128)(2,1)} copy(bf16[2,1,64,512]{3,2,1,0:T(8,128)(2,1)} %get-tuple-element.8) | data formatting | bytes 262144
